TPU v7x, 32 devices: a whole 2x2x4 slice. The times are simulated.
32 devices in a mesh: dp: 16 (over z, y, x), tensor: 2 (over core).
Axes of the slice: x: 2, y: 2, z: 4, core: 2. Of those that a mesh axis runs over, the one named last changes fastest.
Arguments:
- tokens: bfloat16 [16384, 768], P(('dp', 'tensor')), may hold values from -6 to 6
- lengths: int32 [16], P('dp'), may hold values from 1 to 1024, 10240 in all
- qkv_weight: bfloat16 [3, 768, 768], P(None, 'dp', 'tensor'), may hold values from -0.21875 to 0.21875
- qv_bias: float32 [2, 768], P(None, 'tensor'), may hold values from -3 to 3
- out_weight: bfloat16 [768, 768], P('tensor', 'dp'), may hold values from -0.875 to 0.875
- out_bias: float32 [768], replicated, may hold values from -3 to 3
- up_weight: bfloat16 [768, 3072], P('dp', 'tensor'), may hold values from -0.21875 to 0.21875
- up_bias: float32 [3072], P('tensor'), may hold values from -3 to 3
- down_weight: bfloat16 [3072, 768], P('tensor', 'dp'), may hold values from -0.109375 to 0.109375
- down_bias: float32 [768], replicated, may hold values from -3 to 3
- norm1_gain: float32 [768], replicated, may hold values from 0.5 to 1.5
- norm1_shift: float32 [768], replicated, may hold values from -3 to 3
- norm2_gain: float32 [768], replicated, may hold values from 0.5 to 1.5
- norm2_shift: float32 [768], replicated, may hold values from -3 to 3
- cotangent: bfloat16 [16384, 768], P(('dp', 'tensor')), may hold values from -6 to 6
Outputs:
- layer_output: bfloat16 [16384, 768], P(('dp', 'tensor'))
- input_grad: bfloat16 [16384, 768], P(('dp', 'tensor'))
- grad_qkv_weight: float32 [3, 768, 768], P(None, 'dp', 'tensor')
- grad_qv_bias: float32 [2, 768], P(None, 'tensor')
- grad_out_weight: float32 [768, 768], P('tensor', 'dp')
- grad_out_bias: float32 [768], replicated
- grad_up_weight: float32 [768, 3072], P('dp', 'tensor')
- grad_up_bias: float32 [3072], P('tensor')
- grad_down_weight: float32 [3072, 768], P('tensor', 'dp')
- grad_down_bias: float32 [768], replicated
- grad_norm1_gain: float32 [768], replicated
- grad_norm1_shift: float32 [768], replicated
- grad_norm2_gain: float32 [768], replicated
- grad_norm2_shift: float32 [768], replicated
Inputs may be any that keep to these rules, and one draw needn't show every extreme that they name: lengths[s] is the count of real tokens of sequence s; some sequence has 1024.
All inputs are finite; a program needn't handle non-finite values. No bound on the sum of `lengths` on one device may be relied on, other than what follows from the above.
Results may differ from a plain program's by a relative error of at most 0.017.
Values may be sent and summed in bfloat16 or wider, within the bound.
A program may use at most 192 MiB of HBM per device.

v0:
```python
import jax
import jax.numpy as jnp
from jax import lax
from jax.sharding import PartitionSpec as P

HEAD_DIM = 64
LENGTH = 1024
EPSILON = 1e-05
NEGATIVE = -1e30


def layer_norm(values, norm_gain, norm_shift):
    center = values - jnp.mean(values, axis=-1, keepdims=True)
    spread = jnp.mean(center * center, axis=-1, keepdims=True)
    return center * lax.rsqrt(spread + EPSILON) * norm_gain + norm_shift


def gelu_exact(values):
    return jax.nn.gelu(values, approximate=False)


def matmul(left, right):
    return jnp.dot(left, right, preferred_element_type=jnp.float32)


def contract_rows(left, right):
    return lax.dot_general(
        left, right, (((0,), (0,)), ((), ())), preferred_element_type=jnp.float32
    )


def contract_cols(left, right):
    return lax.dot_general(
        left, right, (((1,), (1,)), ((), ())), preferred_element_type=jnp.float32
    )


def per_device(
    tokens,
    lengths,
    qkv_weight,
    qv_bias,
    out_weight,
    out_bias,
    up_weight,
    up_bias,
    down_weight,
    down_bias,
    norm1_gain,
    norm1_shift,
    norm2_gain,
    norm2_shift,
    cotangent,
):
    tok_rows = tokens.shape[0]
    local_width = qkv_weight.shape[2]
    head_count = local_width // HEAD_DIM
    seq_count = lengths.shape[0]
    block_rows = min(512, LENGTH)
    scaling = HEAD_DIM ** (-0.5)
    positions = jnp.arange(LENGTH)
    qkv_full, out_full, up_full, down_full = (
        lax.all_gather(qkv_weight, "dp", axis=1, tiled=True),
        lax.all_gather(out_weight, "dp", axis=1, tiled=True),
        lax.all_gather(up_weight, "dp", axis=0, tiled=True),
        lax.all_gather(down_weight, "dp", axis=1, tiled=True),
    )
    gathered = lax.all_gather(tokens, "tensor", axis=0, tiled=True)
    queries = (matmul(gathered, qkv_full[0]) + qv_bias[0]).astype(jnp.bfloat16)
    key_rows = matmul(gathered, qkv_full[1]).astype(jnp.bfloat16)
    value_rows = (matmul(gathered, qkv_full[2]) + qv_bias[1]).astype(jnp.bfloat16)

    def forward_seq(packed):
        seq_queries, seq_keys, seq_values, length = packed
        query_heads = seq_queries.reshape(LENGTH, head_count, HEAD_DIM)
        key_heads = seq_keys.reshape(LENGTH, head_count, HEAD_DIM)
        value_heads = seq_values.reshape(LENGTH, head_count, HEAD_DIM)
        usable = (positions < length)[None, None, :]
        context_blocks = []
        total_blocks = []
        for block_start in range(0, LENGTH, block_rows):
            block_q = query_heads[block_start : block_start + block_rows]
            scores = (
                jnp.einsum("qhd,khd->hqk", block_q, key_heads, preferred_element_type=jnp.float32)
                * scaling
            )
            scores = jnp.where(usable, scores, NEGATIVE)
            row_top = jnp.max(scores, axis=-1, keepdims=True)
            exponent = jnp.exp(scores - row_top)
            row_total = jnp.sum(exponent, axis=-1, keepdims=True)
            weights = (exponent / row_total).astype(jnp.bfloat16)
            block_context = jnp.einsum(
                "hqk,khd->qhd", weights, value_heads, preferred_element_type=jnp.float32
            )
            context_blocks.append(block_context.reshape(block_rows, local_width))
            total_blocks.append((row_top + jnp.log(row_total))[..., 0])
        return (
            jnp.concatenate(context_blocks, axis=0).astype(jnp.bfloat16),
            jnp.concatenate(total_blocks, axis=1),
        )

    shaped = (
        queries.reshape(seq_count, LENGTH, local_width),
        key_rows.reshape(seq_count, LENGTH, local_width),
        value_rows.reshape(seq_count, LENGTH, local_width),
    )
    contexts, log_totals = lax.map(forward_seq, (shaped[0], shaped[1], shaped[2], lengths))
    context_flat = contexts.reshape(seq_count * LENGTH, local_width)
    row_block = lax.slice_in_dim(context_flat, 0, tok_rows * lax.axis_size("tensor"), axis=0)
    attn = (
        lax.psum_scatter(matmul(row_block, out_full), "tensor", scatter_dimension=0, tiled=True)
        + out_bias
    )
    first_sum = tokens.astype(jnp.float32) + attn
    hidden = layer_norm(first_sum, norm1_gain, norm1_shift)
    hidden_low = hidden.astype(jnp.bfloat16)
    hidden_all = lax.all_gather(hidden_low, "tensor", axis=0, tiled=True)
    upper = matmul(hidden_all, up_full) + up_bias
    active = gelu_exact(upper).astype(jnp.bfloat16)
    row_block = lax.slice_in_dim(active, 0, tok_rows * lax.axis_size("tensor"), axis=0)
    ffn_out = (
        lax.psum_scatter(matmul(row_block, down_full), "tensor", scatter_dimension=0, tiled=True)
        + down_bias
    )
    second_sum = hidden + ffn_out
    layer_output = layer_norm(second_sum, norm2_gain, norm2_shift).astype(jnp.bfloat16)
    qkv_back, out_back, up_back, down_back = (qkv_full, out_full, up_full, down_full)
    unused_two, norm_two_back = jax.vjp(layer_norm, second_sum, norm2_gain, norm2_shift)
    grad_second, gain_two_grad, shift_two_grad = norm_two_back(cotangent.astype(jnp.float32))
    grad_ffn = grad_second.astype(jnp.bfloat16)
    down_bias_grad = jnp.sum(grad_ffn.astype(jnp.float32), axis=0)
    grad_ffn_all = lax.all_gather(grad_ffn, "tensor", axis=0, tiled=True)
    down_weight_grad = contract_rows(active, grad_ffn_all)
    grad_active = contract_cols(grad_ffn_all, down_back)
    unused_gelu, gelu_back = jax.vjp(gelu_exact, upper)
    grad_upper = gelu_back(grad_active)[0].astype(jnp.bfloat16)
    up_bias_grad = jnp.sum(grad_upper.astype(jnp.float32), axis=0)
    up_weight_grad = contract_rows(hidden_all, grad_upper)
    row_block = lax.slice_in_dim(grad_upper, 0, tok_rows * lax.axis_size("tensor"), axis=0)
    grad_hidden = grad_second + lax.psum_scatter(
        contract_cols(row_block, up_back), "tensor", scatter_dimension=0, tiled=True
    )
    unused_one, norm_one_back = jax.vjp(layer_norm, first_sum, norm1_gain, norm1_shift)
    grad_first, gain_one_grad, shift_one_grad = norm_one_back(grad_hidden)
    grad_attn = grad_first.astype(jnp.bfloat16)
    out_bias_grad = jnp.sum(grad_attn.astype(jnp.float32), axis=0)
    grad_attn_all = lax.all_gather(grad_attn, "tensor", axis=0, tiled=True)
    out_weight_grad = contract_rows(context_flat, grad_attn_all)
    grad_context = contract_cols(grad_attn_all, out_back).astype(jnp.bfloat16)

    def backward_seq(packed):
        seq_queries, seq_keys, seq_values, length, seq_grad, seq_totals = packed
        query_heads = seq_queries.reshape(LENGTH, head_count, HEAD_DIM)
        key_heads = seq_keys.reshape(LENGTH, head_count, HEAD_DIM)
        value_heads = seq_values.reshape(LENGTH, head_count, HEAD_DIM)
        usable = (positions < length)[None, None, :]
        key_grad = jnp.zeros((LENGTH, head_count, HEAD_DIM), jnp.float32)
        value_grad = jnp.zeros((LENGTH, head_count, HEAD_DIM), jnp.float32)
        query_blocks = []
        for block_start in range(0, LENGTH, block_rows):
            block_q = query_heads[block_start : block_start + block_rows]
            block_grad = seq_grad[block_start : block_start + block_rows].reshape(
                block_rows, head_count, HEAD_DIM
            )
            scores = (
                jnp.einsum("qhd,khd->hqk", block_q, key_heads, preferred_element_type=jnp.float32)
                * scaling
            )
            scores = jnp.where(usable, scores, NEGATIVE)
            chances = jnp.exp(scores - seq_totals[:, block_start : block_start + block_rows, None])
            weights = chances.astype(jnp.bfloat16)
            value_grad = value_grad + jnp.einsum(
                "hqk,qhd->khd", weights, block_grad, preferred_element_type=jnp.float32
            )
            grad_weights = jnp.einsum(
                "qhd,khd->hqk", block_grad, value_heads, preferred_element_type=jnp.float32
            )
            inner_sum = jnp.sum(grad_weights * chances, axis=-1, keepdims=True)
            grad_scores = (chances * (grad_weights - inner_sum)).astype(jnp.bfloat16)
            block_query_grad = (
                jnp.einsum(
                    "hqk,khd->qhd", grad_scores, key_heads, preferred_element_type=jnp.float32
                )
                * scaling
            )
            query_blocks.append(block_query_grad.reshape(block_rows, local_width))
            key_grad = (
                key_grad
                + jnp.einsum(
                    "hqk,qhd->khd", grad_scores, block_q, preferred_element_type=jnp.float32
                )
                * scaling
            )
        query_grad = jnp.concatenate(query_blocks, axis=0).astype(jnp.bfloat16)
        return (
            query_grad,
            key_grad.reshape(LENGTH, local_width).astype(jnp.bfloat16),
            value_grad.reshape(LENGTH, local_width).astype(jnp.bfloat16),
        )

    grad_shaped = grad_context.reshape(seq_count, LENGTH, local_width)
    query_grads, key_grads, value_grads = lax.map(
        backward_seq, (shaped[0], shaped[1], shaped[2], lengths, grad_shaped, log_totals)
    )
    query_grads = query_grads.reshape(seq_count * LENGTH, local_width)
    key_grads = key_grads.reshape(seq_count * LENGTH, local_width)
    value_grads = value_grads.reshape(seq_count * LENGTH, local_width)
    qv_bias_grad = jnp.stack(
        [
            jnp.sum(query_grads.astype(jnp.float32), axis=0),
            jnp.sum(value_grads.astype(jnp.float32), axis=0),
        ]
    )
    qkv_weight_grad = jnp.stack(
        [
            contract_rows(gathered, query_grads),
            contract_rows(gathered, key_grads),
            contract_rows(gathered, value_grads),
        ]
    )
    part_query = lax.slice_in_dim(query_grads, 0, lax.axis_size("tensor") * tok_rows, axis=0)
    input_grad = (
        grad_first
        + lax.psum_scatter(
            (
                contract_cols(part_query, qkv_back[0])
                + contract_cols(key_grads, qkv_back[1])
                + contract_cols(value_grads, qkv_back[2])
            ).astype(jnp.bfloat16),
            "tensor",
            scatter_dimension=0,
            tiled=True,
        ).astype(jnp.float32)
    ).astype(jnp.bfloat16)
    qkv_grad_own, out_grad_own, up_grad_own, down_grad_own = (
        lax.psum_scatter(qkv_weight_grad, "dp", scatter_dimension=1, tiled=True),
        lax.psum_scatter(out_weight_grad, "dp", scatter_dimension=1, tiled=True),
        lax.psum_scatter(up_weight_grad, "dp", scatter_dimension=0, tiled=True),
        lax.psum_scatter(down_weight_grad, "dp", scatter_dimension=1, tiled=True),
    )
    qv_bias_total, up_bias_total = lax.psum((qv_bias_grad, up_bias_grad), "dp")
    (
        out_bias_total,
        down_bias_total,
        gain_one_total,
        shift_one_total,
        gain_two_total,
        shift_two_total,
    ) = lax.psum(
        (
            out_bias_grad,
            down_bias_grad,
            gain_one_grad,
            shift_one_grad,
            gain_two_grad,
            shift_two_grad,
        ),
        ("dp", "tensor"),
    )
    return (
        layer_output,
        input_grad,
        qkv_grad_own,
        qv_bias_total,
        out_grad_own,
        out_bias_total,
        up_grad_own,
        up_bias_total,
        down_grad_own,
        down_bias_total,
        gain_one_total,
        shift_one_total,
        gain_two_total,
        shift_two_total,
    )


def solution(mesh):
    return jax.shard_map(
        per_device,
        mesh=mesh,
        in_specs=(
            P(("dp", "tensor"), None),
            P("dp"),
            P(None, "dp", "tensor"),
            P(None, "tensor"),
            P("tensor", "dp"),
            P(),
            P("dp", "tensor"),
            P("tensor"),
            P("tensor", "dp"),
            P(),
            P(),
            P(),
            P(),
            P(),
            P(("dp", "tensor"), None),
        ),
        out_specs=(
            P(("dp", "tensor"), None),
            P(("dp", "tensor"), None),
            P(None, "dp", "tensor"),
            P(None, "tensor"),
            P("tensor", "dp"),
            P(),
            P("dp", "tensor"),
            P("tensor"),
            P("tensor", "dp"),
            P(),
            P(),
            P(),
            P(),
            P(),
        ),
        check_vma=False,
    )
```

profile of v0, /device:TPU:0, one launch (start us, length us, event | category | flops | bytes accessed | tf_op | source)
XLA Modules:
  0.0 1038.2 jit_solution(9922317103957784277)
XLA Ops:
  9.4 0.8 slice_reduce_fusion
  10.1 49.1 %all_gather.26 = bf16[384,768]{0,1:T(8,128)(2,1)} all-gather(bf16[384,48]{0,1:T(8,128)(2,1)} %param.19), channel_id=1, replica_groups=mesh['dp'=16,'tensor'=2] {'dp'}, dimensions={1}, use_global_device_ids=true | all-gather | bytes 626688 | tf_op jit(solution)/shard_map/all_gather | solution.py:64
  59.2 25.9 %all-gather.10.cloned.1.call-done = bf16[3,768,384]{2,1,0:T(8,128)(2,1)} async-done(((bf16[3,48,384]{2,1,0:T(8,128)(2,1)}), bf16[3,768,384]{2,1,0:T(8,128)(2,1)}) %all-gather.10.cloned.1.call-update) | async-done | bytes 1769488 | tf_op jit(solution)/shard_map/all_gather | solution.py:63
  85.1 2.4 add_convert_fusion.5
  87.6 2.2 convolution_convert_fusion.1
  89.8 1.8 fusion.56
  91.6 4.9 fusion.18
  96.6 5.6 fusion
  102.2 1.9 add_convert_fusion.6
  104.2 3.8 fusion.30
  108.0 3.8 fusion.29
  112.5 2.7 fusion.34
  115.9 9.2 reduce-scatter.8.cloned.1.call-done
  125.1 1.7 fusion.53
  127.1 1.2 fusion.26
  129.2 62.5 %all-gather.14.cloned.1.call-done = bf16[768,1536]{1,0:T(8,128)(2,1)} async-done(((bf16[48,1536]{1,0:T(8,128)(2,1)}), bf16[768,1536]{1,0:T(8,128)(2,1)}) %all-gather.14.cloned.1.call-update) | async-done | bytes 2359312 | tf_op jit(solution)/shard_map/all_gather | solution.py:65
  191.6 10.7 %all-gather.12.cloned.1.call-done = bf16[1024,768]{1,0:T(8,128)(2,1)} async-done(((bf16[512,768]{1,0:T(8,128)(2,1)}), bf16[1024,768]{1,0:T(8,128)(2,1)}) %all-gather.12.cloned.1.call-update) | async-done | bytes 1572880 | tf_op jit(solution)/shard_map/all_gather | solution.py:117
  202.3 19.9 %multiply_convert_fusion.2 = (bf16[1024,1536]{1,0:T(8,128)(2,1)}, f32[1024,1536]{1,0:T(8,128)}, f32[1024,1536]{1,0:T(8,128)}) fusion(f32[1536]{0:T(1024)S(1)} %copy-done.44, bf16[1024,768]{1,0:T(8,128)(2,1)} %all-gather.12.cloned.1.call-done, bf16[768,1536]{1,0:T(8,128)(2,1)} %all-gather.14.cloned.1.call-done), kind=kOutput, calls=%fused_computation.24 | convolution fusion | flops 2519728128 | bytes 19666944 | tf_op jit(solution)/shard_map/dot_general | solution.py:23
  222.2 46.7 %all-gather.16.cloned.1.call-done = bf16[1536,768]{0,1:T(8,128)(2,1)} async-done(((bf16[1536,48]{0,1:T(8,128)(2,1)}), bf16[1536,768]{0,1:T(8,128)(2,1)}) %all-gather.16.cloned.1.call-update) | async-done | bytes 2359312 | tf_op jit(solution)/shard_map/all_gather | solution.py:66
  268.8 6.9 fusion.57
  275.8 9.8 reduce-scatter.10.cloned.1.call-done
  285.6 2.0 fusion.51
  288.7 1.6 fusion.50
  290.3 1.1 convert_reduce_fusion.2
  291.5 11.1 %all-gather.18.cloned.1.call-done = bf16[1024,768]{1,0:T(8,128)(2,1)} async-done(((bf16[512,768]{1,0:T(8,128)(2,1)}), bf16[1024,768]{1,0:T(8,128)(2,1)}) %all-gather.18.cloned.1.call-update) | async-done | bytes 1572880 | tf_op jit(solution)/shard_map/all_gather | solution.py:132
  302.5 10.9 %convert_reduce_fusion = (f32[1536]{0:T(1024)}, bf16[1024,1536]{1,0:T(8,128)(2,1)S(1)}) fusion(f32[1024,1536]{1,0:T(8,128)} %get-tuple-element.135, f32[1024,1536]{1,0:T(8,128)} %get-tuple-element.146, f32[1536]{0:T(1024)S(1)} %copy-done.44, bf16[1024,768]{1,0:T(8,128)(2,1)} %all-gather.18.cloned.1.call-done, ...), kind=kOutput, calls=%fused_computation.20 | convolution fusion | flops 2442656256 | bytes 19673088 | tf_op jit(solution)/shard_map/dot_general | solution.py:33
  313.5 1.6 copy-done.17
  315.1 4.4 fusion.58
  319.5 12.2 %reduce-scatter.12.cloned.1.call-done = f32[512,768]{1,0:T(8,128)} async-done(((f32[1024,768]{1,0:T(8,128)}), f32[512,768]{1,0:T(8,128)}) %reduce-scatter.12.cloned.1.call-update) | async-done | bytes 1572880 | tf_op jit(solution)/shard_map/reduce_scatter | solution.py:140
  331.7 2.8 multiply_reduce_fusion.2
  335.2 1.1 copy-done.2
  336.3 1.7 convert_reduce_fusion.3
  338.5 10.6 %all-gather.20.cloned.1.call-done = bf16[1024,768]{1,0:T(8,128)(2,1)} async-done(((bf16[512,768]{1,0:T(8,128)(2,1)}), bf16[1024,768]{1,0:T(8,128)(2,1)}) %all-gather.20.cloned.1.call-update) | async-done | bytes 1572880 | tf_op jit(solution)/shard_map/all_gather | solution.py:147
  349.1 2.2 convolution_convert_fusion
  351.4 6.4 fusion.59
  357.9 7.3 fusion.5
  365.1 18.9 %multiply_reduce_fusion.1 = (f32[6,512]{1,0:T(8,128)S(1)}, f32[6,512]{1,0:T(8,128)S(1)}, f32[6,512,1024]{2,1,0:T(8,128)}) fusion(f32[6,512]{1,0:T(8,128)S(1)} %get-tuple-element.151, f32[6,512,1024]{2,1,0:T(8,128)} %copy-done.1, pred[1024]{0:T(1024)(128)(4,1)S(1)} %iota_compare_fusion, f32[6,512,1024]{2,1,0:T(8,128)} %fusion.59, ...), kind=kOutput, calls=%fused_computation.4 | convolution fusion | flops 434104320 | bytes 51561472 | tf_op jit(solution)/shard_map/while/body/eval_jaxpr/qhd,khd->hqk/dot_general | solution.py:175
  384.1 17.3 %multiply_convert_fusion.1 = (bf16[6,512,1024]{2,1,0:T(8,128)(2,1)S(1)}, bf16[6,512,1024]{2,1,0:T(8,128)(2,1)S(1)}) fusion(f32[6,512,1024]{2,1,0:T(8,128)} %get-tuple-element.147, f32[6,512]{1,0:T(8,128)S(1)} %get-tuple-element.107, f32[6,512]{1,0:T(8,128)S(1)} %get-tuple-element.151, f32[6,512,1024]{2,1,0:T(8,128)} %copy-done.1, ...), kind=kLoop, calls=%fused_computation.3 | loop fusion | flops 37748736 | bytes 62964736 | tf_op jit(solution)/shard_map/while/body/eval_jaxpr/convert_element_type | solution.py:179
  401.4 2.0 fusion.27
  403.5 1.2 fusion.60
  405.0 7.2 convert_reduce_fusion.4
  412.2 2.0 fusion.28
  414.3 1.3 multiply_convert_fusion.3
  415.9 1.0 fusion.32
  416.9 1.0 fusion.31
  417.9 2.2 add_convert_fusion.1
  420.2 2.3 convolution_bitcast_fusion.2
  422.5 0.8 convolution_bitcast_fusion
  423.3 0.8 convolution_bitcast_fusion.1
  424.3 4.1 copy.30
  428.5 1.4 copy-done.43
  429.9 6.3 fusion.62
  436.3 1.8 copy-done.18
  438.1 5.8 fusion.61
  444.0 0.8 copy-done.25
  445.0 3.5 fusion.33
  449.8 43.9 %all-reduce.1 = (f32[768]{0:T(1024)}, f32[768]{0:T(1024)}, f32[768]{0:T(1024)}, f32[768]{0:T(1024)}, f32[768]{0:T(1024)}, /*index=5*/f32[768]{0:T(1024)}) all-reduce(f32[768]{0:T(1024)S(1)} %copy-done.30, f32[768]{0:T(1024)S(1)} %get-tuple-element.121, f32[768]{0:T(1024)S(1)} %copy-done.32, ...), channel_id=1, replica_groups=mesh['dp'=16,'tensor'=2] {'dp','tensor'}, use_global_device_ids=true, to_apply=%region_24.25 | all-reduce | flops 4608 | bytes 36864 | tf_op jit(solution)/shard_map/psum | solution.py:249
  494.0 76.4 %all-reduce.2 = (f32[2,384]{1,0:T(2,128)}, f32[1536]{0:T(1024)}) all-reduce(f32[2,384]{1,0:T(2,128)S(1)} %pad_maximum_fusion.7, f32[1536]{0:T(1024)S(1)} %copy-done.34), channel_id=1, replica_groups=mesh['dp'=16,'tensor'=2] {'dp'}, use_global_device_ids=true, to_apply=%region_21.22 | all-reduce | flops 2304 | bytes 18432 | tf_op jit(solution)/shard_map/psum | solution.py:241
  570.5 2.3 add_convert_fusion.2
  572.7 45.6 %all-reduce.5.cloned.1.call-done = f32[3,768,384]{2,0,1:T(4,128)} async-done(((f32[3,768,384]{2,0,1:T(4,128)}), f32[3,768,384]{2,0,1:T(4,128)}) %all-reduce.5.cloned.1.call-update) | async-done | bytes 3538960
  618.3 1.0 constant_dynamic-slice_fusion
  620.1 141.2 %reduce-scatter.20.cloned.1.call-done = f32[1536,48]{0,1:T(8,128)} async-done(((f32[1536,768]{0,1:T(8,128)}), f32[1536,48]{0,1:T(8,128)}) %reduce-scatter.20.cloned.1.call-update) | async-done | bytes 294928 | tf_op jit(solution)/shard_map/reduce_scatter | solution.py:239
  761.2 141.7 %reduce-scatter.18.cloned.1.call-done = f32[48,1536]{1,0:T(8,128)} async-done(((f32[768,1536]{1,0:T(8,128)}), f32[48,1536]{1,0:T(8,128)}) %reduce-scatter.18.cloned.1.call-update) | async-done | bytes 294928 | tf_op jit(solution)/shard_map/reduce_scatter | solution.py:238
  902.9 128.6 %reduce-scatter.16.cloned.1.call-done = f32[384,48]{0,1:T(8,128)} async-done(((f32[384,768]{0,1:T(8,128)}), f32[384,48]{0,1:T(8,128)}) %reduce-scatter.16.cloned.1.call-update) | async-done | bytes 73744 | tf_op jit(solution)/shard_map/reduce_scatter | solution.py:237
  (144 shorter events, 9.4 us)
Async XLA Ops:
  7.2 52.0 %all-gather.8.cloned.1.call-start = ((), (), s32[]{:S(2)}) async-start(), calls=%async_computation.7 | async-start | bytes 2359296 | tf_op jit(solution)/shard_map/all_gather | solution.py:68
  7.9 77.2 %all-gather.10.cloned.1.call-start = ((), (), s32[]{:S(2)}) async-start(), calls=%async_computation.8 | async-start | bytes 1880064 | tf_op jit(solution)/shard_map/all_gather | solution.py:63
  8.7 116.4 %reduce-scatter.8.cloned.1.call-start = ((), (), s32[]{:S(2)}) async-start(), calls=%async_computation.9 | async-start | bytes 4718592 | tf_op jit(solution)/shard_map/reduce_scatter | solution.py:111
  59.2 28.3 %copy-start.40 = (bf16[1024,768]{1,0:T(8,128)(2,1)S(1)}, bf16[1024,768]{1,0:T(8,128)(2,1)}, u32[]{:S(2)}) copy-start(bf16[1024,768]{1,0:T(8,128)(2,1)} %all-gather.8.cloned.1.call-done) | copy-start | bytes 4718596
  87.6 4.1 copy-start.6
  87.6 4.1 copy-start.8
  89.8 1.9 copy-start.4
  91.6 16.3 %copy-start = (f32[6,512,1024]{2,1,0:T(8,128)}, f32[6,512,1024]{2,1,0:T(8,128)S(1)}, u32[]{:S(2)}) copy-start(f32[6,512,1024]{2,1,0:T(8,128)S(1)} %fusion.56) | copy-start | bytes 37748740
  96.5 7.6 copy-start.1
  96.6 5.7 copy-start.41
  104.1 3.8 copy-start.19
  107.9 3.8 copy-start.24
  108.0 4.5 copy-start.21
  111.8 0.7 copy-start.26
  112.5 12.6 %copy-start.16 = (bf16[512,768]{1,0:T(8,128)(2,1)S(1)}, bf16[512,768]{1,0:T(8,128)(2,1)}, u32[]{:S(2)}) copy-start(bf16[512,768]{1,0:T(8,128)(2,1)} %param.15) | copy-start | bytes 2359300
  112.5 12.6 %copy-start.37 = (f32[768]{0:T(1024)S(1)}, f32[768]{0:T(1024)}, u32[]{:S(2)}) copy-start(f32[768]{0:T(1024)} %param.20) | copy-start | bytes 9220
  115.3 11.8 %copy-start.28 = (f32[768]{0:T(1024)S(1)}, f32[768]{0:T(1024)}, u32[]{:S(2)}) copy-start(f32[768]{0:T(1024)} %param.25) | copy-start | bytes 9220
  115.3 11.8 %copy-start.31 = (f32[768]{0:T(1024)S(1)}, f32[768]{0:T(1024)}, u32[]{:S(2)}) copy-start(f32[768]{0:T(1024)} %param.26) | copy-start | bytes 9220
  115.3 76.3 %all-gather.14.cloned.1.call-start = ((), (), s32[]{:S(2)}) async-start(), calls=%async_computation.11 | async-start | bytes 2506752 | tf_op jit(solution)/shard_map/all_gather | solution.py:65
  115.9 86.4 %all-gather.12.cloned.1.call-start = ((), (), s32[]{:S(2)}) async-start(), calls=%async_computation.10 | async-start | bytes 2359296 | tf_op jit(solution)/shard_map/all_gather | solution.py:117
  126.8 75.5 %copy-start.44 = (f32[1536]{0:T(1024)S(1)}, f32[1536]{0:T(1024)}, u32[]{:S(2)}) copy-start(f32[1536]{0:T(1024)} %param.22) | copy-start | bytes 18436
  128.4 140.5 %all-gather.16.cloned.1.call-start = ((), (), s32[]{:S(2)}) async-start(), calls=%async_computation.12 | async-start | bytes 2506752 | tf_op jit(solution)/shard_map/all_gather | solution.py:66
  128.9 156.7 %reduce-scatter.10.cloned.1.call-start = ((), (), s32[]{:S(2)}) async-start(), calls=%async_computation.13 | async-start | bytes 4718592 | tf_op jit(solution)/shard_map/reduce_scatter | solution.py:122
  275.7 9.9 copy-start.38
  275.7 12.2 %copy-start.14 = (bf16[512,768]{1,0:T(8,128)(2,1)S(1)}, bf16[512,768]{1,0:T(8,128)(2,1)}, u32[]{:S(2)}) copy-start(bf16[512,768]{1,0:T(8,128)(2,1)} %param.29) | copy-start | bytes 2359300
  275.8 12.2 %copy-start.29 = (f32[768]{0:T(1024)S(1)}, f32[768]{0:T(1024)}, u32[]{:S(2)}) copy-start(f32[768]{0:T(1024)} %param.27) | copy-start | bytes 9220
  275.8 26.8 %all-gather.18.cloned.1.call-start = ((), (), s32[]{:S(2)}) async-start(), calls=%async_computation.14 | async-start | bytes 2359296 | tf_op jit(solution)/shard_map/all_gather | solution.py:132
  287.6 1.1 copy-start.15
  287.6 1.1 copy-start.35
  291.4 40.3 %reduce-scatter.12.cloned.1.call-start = ((), (), s32[]{:S(2)}) async-start(), calls=%async_computation.15 | async-start | bytes 4718592 | tf_op jit(solution)/shard_map/reduce_scatter | solution.py:140
  302.5 12.5 %copy-start.39 = (bf16[768,1536]{1,0:T(8,128)(2,1)S(1)}, bf16[768,1536]{1,0:T(8,128)(2,1)}, u32[]{:S(2)}) copy-start(bf16[768,1536]{1,0:T(8,128)(2,1)} %all-gather.14.cloned.1.call-done) | copy-start | bytes 7077892
  313.5 1.6 copy-start.17
  319.5 29.7 %all-gather.20.cloned.1.call-start = ((), (), s32[]{:S(2)}) async-start(), calls=%async_computation.16 | async-start | bytes 2359296 | tf_op jit(solution)/shard_map/all_gather | solution.py:147
  334.5 14.6 %copy-start.22 = (bf16[384,768]{0,1:T(8,128)(2,1)S(1)}, bf16[384,768]{0,1:T(8,128)(2,1)}, u32[]{:S(2)}) copy-start(bf16[384,768]{0,1:T(8,128)(2,1)} %all_gather.26) | copy-start | bytes 1769476
  335.2 1.1 copy-start.2
  338.0 13.4 %copy-start.20 = (bf16[1024,384]{0,1:T(8,128)(2,1)S(1)}, bf16[1024,384]{0,1:T(8,128)(2,1)}, u32[]{:S(2)}) copy-start(bf16[1024,384]{0,1:T(8,128)(2,1)} %copy-done.19) | copy-start | bytes 2359300
  338.0 232.5 %reduce-scatter.14.cloned.1.call-start = ((), (), s32[]{:S(2)}) async-start(), calls=%async_computation.17 | async-start | bytes 2359296 | tf_op jit(solution)/shard_map/reduce_scatter | solution.py:224
  384.1 17.3 %copy-start.5 = (bf16[1024,384]{0,1:T(8,128)(2,1)S(1)}, bf16[1024,384]{0,1:T(8,128)(2,1)}, u32[]{:S(2)}) copy-start(bf16[1024,384]{0,1:T(8,128)(2,1)} %copy-done.4) | copy-start | bytes 2359300
  401.4 2.0 copy-start.9
  403.5 16.7 %copy-start.10 = (bf16[6,64,512]{2,1,0:T(8,128)(2,1)}, bf16[6,64,512]{2,1,0:T(8,128)(2,1)S(1)}, u32[]{:S(2)}) copy-start(bf16[6,64,512]{2,1,0:T(8,128)(2,1)S(1)} %fusion.27) | copy-start | bytes 1179652
  403.5 1.6 copy-start.46
  412.2 2.0 copy-start.7
  414.3 6.0 copy-start.12
  414.3 1.6 copy-start.23
  420.2 198.2 %all-reduce.5.cloned.1.call-start = ((), (), s32[]{:S(2)}) async-start(), calls=%async_computation.21 | async-start | bytes 9437184
  420.2 2.3 copy-start.42
  428.4 1.5 copy-start.43
  428.4 332.8 %reduce-scatter.20.cloned.1.call-start = ((), (), s32[]{:S(2)}) async-start(), calls=%async_computation.20 | async-start | bytes 5013504 | tf_op jit(solution)/shard_map/reduce_scatter | solution.py:239
  436.2 1.9 copy-start.18
  436.2 466.7 %reduce-scatter.18.cloned.1.call-start = ((), (), s32[]{:S(2)}) async-start(), calls=%async_computation.19 | async-start | bytes 5013504 | tf_op jit(solution)/shard_map/reduce_scatter | solution.py:238
  443.9 1.0 copy-start.25
  443.9 1.1 copy-start.27
  443.9 4.6 copy-start.45
  443.9 5.9 copy-start.30
  443.9 5.9 copy-start.32
  443.9 5.9 copy-start.33
  443.9 49.8 %copy-start.36 = (f32[6,64]{1,0:T(8,128)S(1)}, f32[6,64]{1,0:T(8,128)}, u32[]{:S(2)}) copy-start(f32[6,64]{1,0:T(8,128)} %get-tuple-element.148) | copy-start | bytes 4612
  443.9 49.9 %copy-start.11 = (bf16[6,64,512]{2,1,0:T(8,128)(2,1)S(1)}, bf16[6,64,512]{2,1,0:T(8,128)(2,1)}, u32[]{:S(2)}) copy-start(bf16[6,64,512]{2,1,0:T(8,128)(2,1)} %copy-done.10) | copy-start | bytes 1179652
  444.0 49.8 %copy-start.13 = (bf16[6,64,512]{2,1,0:T(8,128)(2,1)S(1)}, bf16[6,64,512]{2,1,0:T(8,128)(2,1)}, u32[]{:S(2)}) copy-start(bf16[6,64,512]{2,1,0:T(8,128)(2,1)} %copy-done.12) | copy-start | bytes 1179652
  444.0 50.0 %copy-start.34 = (f32[1536]{0:T(1024)S(1)}, f32[1536]{0:T(1024)}, u32[]{:S(2)}) copy-start(f32[1536]{0:T(1024)} %get-tuple-element.125) | copy-start | bytes 18436
  444.0 126.5 %copy-start.3 = (f32[512,768]{1,0:T(8,128)S(1)}, f32[512,768]{1,0:T(8,128)}, u32[]{:S(2)}) copy-start(f32[512,768]{1,0:T(8,128)} %copy-done.2) | copy-start | bytes 4718596
  444.0 587.5 %reduce-scatter.16.cloned.1.call-start = ((), (), s32[]{:S(2)}) async-start(), calls=%async_computation.18 | async-start | bytes 1253376 | tf_op jit(solution)/shard_map/reduce_scatter | solution.py:237
Sparse Core Ops, SparseCore 0:
  9.6 12.4 all-gather.7
  24.8 60.2 all-gather.9
  115.4 9.6 reduce-scatter.7
  128.1 63.4 all-gather.13
  193.7 8.6 all-gather.11
  205.3 63.4 all-gather.15
  275.9 9.7 reduce-scatter.9
  291.5 10.9 all-gather.17
  319.6 12.0 reduce-scatter.11
  338.1 10.9 all-gather.19
  420.3 10.2 reduce-scatter.13
  436.1 182.1 all-reduce.4
  624.9 136.2 reduce-scatter.19
  766.8 136.0 reduce-scatter.17
  908.8 122.6 reduce-scatter.15
where the time goes:
time: 1050 us; the launch traced here: 1040 us
  waiting for transfers between devices  658 us (63%)
  blocking collectives  169 us (16%)
  matrix products  138 us (13%)
  other arithmetic  39.6 us (4%)
  between operations  16.1 us (2%)
  local copies, waits for them, and re-layouts  15.8 us (2%)
    reduce_scatter x1, waiting for transfers between devices, per_device(): lax.psum_scatter(up_weight_grad, 'dp', scatter_dimension=0, tiled=True)  142 us
    reduce_scatter x1, waiting for transfers between devices, per_device(): lax.psum_scatter(down_weight_grad, 'dp', scatter_dimension=1, tiled=True)  141 us
    reduce_scatter x1, waiting for transfers between devices, per_device(): lax.psum_scatter(out_weight_grad, 'dp', scatter_dimension=1, tiled=True)  129 us
    psum x1, blocking collectives, per_device(): qv_bias_total, up_bias_total = lax.psum((qv_bias_grad, up_bias_grad), 'dp')  76.4 us
    all_gather x1, waiting for transfers between devices, per_device(): lax.all_gather(up_weight, 'dp', axis=0, tiled=True)  62.5 us
    all_gather x1, blocking collectives, per_device(): lax.all_gather(out_weight, 'dp', axis=1, tiled=True)  49.1 us
    unnamed x16, waiting for transfers between devices  48.2 us
    all_gather x1, waiting for transfers between devices, per_device(): lax.all_gather(down_weight, 'dp', axis=1, tiled=True)  46.7 us
  transfers between devices with their start and end apart: 15, of which 13 were waited for; matrix products, arithmetic and copies ran while one was open for 5% of the time, Pallas kernels for 0%

commit v1 on v0

--- a/solution.py
+++ b/solution.py
@@ -59,8 +59,22 @@
     block_rows = min(512, LENGTH)
     scaling = HEAD_DIM ** (-0.5)
     positions = jnp.arange(LENGTH)
+
+    def update_the_arrays(raw):
+        across = "dp"
+        v1 = jax.lax.axis_size(across)
+        side_arr, e_next, prior = (v1, jax.lax.axis_index(across), raw.shape[1])
+        spare, aux = (raw, 1)
+        while aux < side_arr:
+            all_rows = []
+            for c in range(side_arr):
+                all_rows.append((c, (c - aux) % side_arr))
+            spare = jnp.concatenate([spare, jax.lax.ppermute(spare, across, all_rows)], axis=1)
+            aux = 2 * aux
+        return jnp.roll(spare, e_next * prior, axis=1)
+
     qkv_full, out_full, up_full, down_full = (
-        lax.all_gather(qkv_weight, "dp", axis=1, tiled=True),
+        update_the_arrays(qkv_weight),
         lax.all_gather(out_weight, "dp", axis=1, tiled=True),
         lax.all_gather(up_weight, "dp", axis=0, tiled=True),
         lax.all_gather(down_weight, "dp", axis=1, tiled=True),

time: 1050 us -> 948 us (0.903)
  waiting for transfers between devices: 658 us -> 522 us
  blocking collectives: 169 us -> 183 us
    reduce_scatter x1, waiting for transfers between devices: 141 us -> 8.55 us  [per_device(): lax.psum_scatter(down_weight_grad, 'dp', scatter_dimension=1, tiled=True)]
    all_gather x1 -> x0, waiting for transfers between devices: 25.9 us -> none  [per_device(): lax.all_gather(qkv_weight, 'dp', axis=1, tiled=True)]
    ppermute x0 -> x4, waiting for transfers between devices: none -> 17.1 us  [update_the_arrays(): jax.lax.ppermute(spare, across, all_rows)]
    all_gather x1, blocking collectives: 49.1 us -> 62.3 us  [per_device(): lax.all_gather(out_weight, 'dp', axis=1, tiled=True)]
    all_gather x1, waiting for transfers between devices: 62.5 us -> 51.2 us  [per_device(): lax.all_gather(up_weight, 'dp', axis=0, tiled=True)]
    unnamed x16 -> x15, waiting for transfers between devices: 48.2 us -> 56 us
  transfers between devices with their start and end apart: 15 -> 18, of which waited for: 13 -> 15; matrix products, arithmetic and copies ran while one was open for 5% -> 6% of each run, Pallas kernels for 0% -> 0%
where the time goes in v1:
time: 948 us; the launch traced here: 939 us
  waiting for transfers between devices  522 us (55%)
  blocking collectives  183 us (19%)
  matrix products  139 us (15%)
  other arithmetic  43.7 us (5%)
  local copies, waits for them, and re-layouts  23.1 us (2%)
  between operations  18 us (2%)
  starting transfers between devices  10 us (1%)
    reduce_scatter x1, waiting for transfers between devices, per_device(): lax.psum_scatter(up_weight_grad, 'dp', scatter_dimension=0, tiled=True)  142 us
    reduce_scatter x1, waiting for transfers between devices, per_device(): lax.psum_scatter(out_weight_grad, 'dp', scatter_dimension=1, tiled=True)  129 us
    psum x1, blocking collectives, per_device(): qv_bias_total, up_bias_total = lax.psum((qv_bias_grad, up_bias_grad), 'dp')  76.6 us
    all_gather x1, blocking collectives, per_device(): lax.all_gather(out_weight, 'dp', axis=1, tiled=True)  62.3 us
    unnamed x15, waiting for transfers between devices  56 us
    all_gather x1, waiting for transfers between devices, per_device(): lax.all_gather(up_weight, 'dp', axis=0, tiled=True)  51.2 us
    all_gather x1, waiting for transfers between devices, per_device(): lax.all_gather(down_weight, 'dp', axis=1, tiled=True)  46.7 us
    psum x1, blocking collectives, per_device(): lax.psum((out_bias_grad, down_bias_grad, gain_one_grad, shift_one_grad, g...  43.9 us
  transfers between devices with their start and end apart: 18, of which 15 were waited for; matrix products, arithmetic and copies ran while one was open for 6% of the time, Pallas kernels for 0%

profile of v1, /device:TPU:0, one launch (start us, length us, event | category | flops | bytes accessed | tf_op | source)
XLA Modules:
  0.0 938.8 jit_solution(16854281557498533310)
XLA Ops:
  8.1 7.0 collective-permute-start
  15.1 2.6 collective-permute-done
  18.6 1.5 collective-permute-start.1
  20.1 4.9 collective-permute-done.1
  26.5 9.6 %collective-permute-done.2 = bf16[3,192,384]{2,1,0:T(8,128)(2,1)S(1)} collective-permute-done((bf16[3,192,384]{2,1,0:T(8,128)(2,1)S(1)}, bf16[3,192,384]{2,1,0:T(8,128)(2,1)S(1)}, u32[]{:S(2)}, u32[]{:S(2)}) %collective-permute-start.2) | collective-permute-done | bytes 442400 | tf_op jit(solution)/shard_map/ppermute | solution.py:72
  38.6 62.3 %all_gather.22 = bf16[384,768]{0,1:T(8,128)(2,1)} all-gather(bf16[384,48]{0,1:T(8,128)(2,1)S(1)} %copy-done.28), channel_id=1, replica_groups=mesh['dp'=16,'tensor'=2] {'dp'}, dimensions={1}, use_global_device_ids=true | all-gather | bytes 626688 | tf_op jit(solution)/shard_map/all_gather | solution.py:78
  107.0 1.0 constant_dynamic-update-slice_fusion
  108.0 2.5 fusion.26
  110.6 2.2 convolution_convert_fusion.1
  112.8 1.8 fusion.64
  114.7 4.9 fusion.18
  119.6 5.6 fusion
  125.3 1.9 add_convert_fusion.6
  127.3 3.8 fusion.31
  131.1 3.8 fusion.30
  135.6 2.7 fusion.36
  139.0 18.9 %reduce-scatter.8.cloned.1.call-done = f32[512,768]{1,0:T(8,128)} async-done(((f32[1024,768]{1,0:T(8,128)}), f32[512,768]{1,0:T(8,128)}) %reduce-scatter.8.cloned.1.call-update) | async-done | bytes 1572880 | tf_op jit(solution)/shard_map/reduce_scatter | solution.py:125
  158.0 1.7 fusion.61
  160.0 1.2 fusion.27
  161.9 51.2 %all-gather.11.cloned.1.call-done = bf16[768,1536]{1,0:T(8,128)(2,1)} async-done(((bf16[48,1536]{1,0:T(8,128)(2,1)}), bf16[768,1536]{1,0:T(8,128)(2,1)}) %all-gather.11.cloned.1.call-update) | async-done | bytes 2359312 | tf_op jit(solution)/shard_map/all_gather | solution.py:79
  213.1 10.0 %all-gather.9.cloned.1.call-done = bf16[1024,768]{1,0:T(8,128)(2,1)} async-done(((bf16[512,768]{1,0:T(8,128)(2,1)}), bf16[1024,768]{1,0:T(8,128)(2,1)}) %all-gather.9.cloned.1.call-update) | async-done | bytes 1572880 | tf_op jit(solution)/shard_map/all_gather | solution.py:131
  223.2 20.1 %multiply_convert_fusion.2 = (bf16[1024,1536]{1,0:T(8,128)(2,1)}, f32[1024,1536]{1,0:T(8,128)}, f32[1024,1536]{1,0:T(8,128)}) fusion(f32[1536]{0:T(1024)S(1)} %copy-done.45, bf16[1024,768]{1,0:T(8,128)(2,1)} %all-gather.9.cloned.1.call-done, bf16[768,1536]{1,0:T(8,128)(2,1)} %all-gather.11.cloned.1.call-done), kind=kOutput, calls=%fused_computation.24 | convolution fusion | flops 2519728128 | bytes 19666944 | tf_op jit(solution)/shard_map/dot_general | solution.py:23
  243.2 46.7 %all-gather.13.cloned.1.call-done = bf16[1536,768]{0,1:T(8,128)(2,1)} async-done(((bf16[1536,48]{0,1:T(8,128)(2,1)}), bf16[1536,768]{0,1:T(8,128)(2,1)}) %all-gather.13.cloned.1.call-update) | async-done | bytes 2359312 | tf_op jit(solution)/shard_map/all_gather | solution.py:80
  290.0 6.9 fusion.65
  297.0 9.2 reduce-scatter.10.cloned.1.call-done
  306.2 2.0 fusion.59
  309.3 2.7 fusion.58
  312.0 1.1 convert_reduce_fusion.2
  313.4 10.7 %all-gather.15.cloned.1.call-done = bf16[1024,768]{1,0:T(8,128)(2,1)} async-done(((bf16[512,768]{1,0:T(8,128)(2,1)}), bf16[1024,768]{1,0:T(8,128)(2,1)}) %all-gather.15.cloned.1.call-update) | async-done | bytes 1572880 | tf_op jit(solution)/shard_map/all_gather | solution.py:146
  324.1 10.9 %convert_reduce_fusion = (f32[1536]{0:T(1024)}, bf16[1024,1536]{1,0:T(8,128)(2,1)S(1)}) fusion(f32[1024,1536]{1,0:T(8,128)} %get-tuple-element.135, f32[1024,1536]{1,0:T(8,128)} %get-tuple-element.146, f32[1536]{0:T(1024)S(1)} %copy-done.45, bf16[1024,768]{1,0:T(8,128)(2,1)} %all-gather.15.cloned.1.call-done, ...), kind=kOutput, calls=%fused_computation.20 | convolution fusion | flops 2442656256 | bytes 19673088 | tf_op jit(solution)/shard_map/dot_general | solution.py:33
  335.0 1.7 copy-done.16
  336.7 4.4 fusion.66
  341.1 12.0 %reduce-scatter.12.cloned.1.call-done = f32[512,768]{1,0:T(8,128)} async-done(((f32[1024,768]{1,0:T(8,128)}), f32[512,768]{1,0:T(8,128)}) %reduce-scatter.12.cloned.1.call-update) | async-done | bytes 1572880 | tf_op jit(solution)/shard_map/reduce_scatter | solution.py:154
  353.1 2.8 multiply_reduce_fusion.2
  356.6 1.2 copy-done.2
  357.8 1.7 convert_reduce_fusion.3
  359.5 11.1 %all-gather.17.cloned.1.call-done = bf16[1024,768]{1,0:T(8,128)(2,1)} async-done(((bf16[512,768]{1,0:T(8,128)(2,1)}), bf16[1024,768]{1,0:T(8,128)(2,1)}) %all-gather.17.cloned.1.call-update) | async-done | bytes 1572880 | tf_op jit(solution)/shard_map/all_gather | solution.py:161
  370.7 2.2 convolution_convert_fusion
  373.0 6.4 fusion.67
  379.4 7.7 fusion.5
  387.1 19.0 %multiply_reduce_fusion.1 = (f32[6,512]{1,0:T(8,128)S(1)}, f32[6,512]{1,0:T(8,128)S(1)}, f32[6,512,1024]{2,1,0:T(8,128)}) fusion(f32[6,512]{1,0:T(8,128)S(1)} %get-tuple-element.151, f32[6,512,1024]{2,1,0:T(8,128)} %copy-done.1, pred[1024]{0:T(1024)(128)(4,1)S(1)} %iota_compare_fusion, f32[6,512,1024]{2,1,0:T(8,128)} %fusion.67, ...), kind=kOutput, calls=%fused_computation.4 | convolution fusion | flops 434104320 | bytes 51561472 | tf_op jit(solution)/shard_map/while/body/eval_jaxpr/qhd,khd->hqk/dot_general | solution.py:189
  406.1 17.3 %multiply_convert_fusion.1 = (bf16[6,512,1024]{2,1,0:T(8,128)(2,1)S(1)}, bf16[6,512,1024]{2,1,0:T(8,128)(2,1)S(1)}) fusion(f32[6,512,1024]{2,1,0:T(8,128)} %get-tuple-element.147, f32[6,512]{1,0:T(8,128)S(1)} %get-tuple-element.107, f32[6,512]{1,0:T(8,128)S(1)} %get-tuple-element.151, f32[6,512,1024]{2,1,0:T(8,128)} %copy-done.1, ...), kind=kLoop, calls=%fused_computation.3 | loop fusion | flops 37748736 | bytes 62964736 | tf_op jit(solution)/shard_map/while/body/eval_jaxpr/convert_element_type | solution.py:193
  423.4 2.0 fusion.28
  425.5 1.2 fusion.68
  426.7 2.0 fusion.29
  429.7 4.0 convert_reduce_fusion.4
  433.6 1.2 multiply_convert_fusion.3
  434.8 2.1 fusion.34
  436.9 2.1 fusion.32
  439.1 3.3 add_convert_fusion.1
  442.5 2.3 convolution_bitcast_fusion.2
  446.6 4.0 copy.30
  450.7 1.4 copy-done.44
  452.1 6.4 fusion.70
  458.6 1.9 copy-done.17
  460.4 5.8 fusion.69
  467.3 3.6 fusion.35
  472.3 43.9 %all-reduce.1 = (f32[768]{0:T(1024)}, f32[768]{0:T(1024)}, f32[768]{0:T(1024)}, f32[768]{0:T(1024)}, f32[768]{0:T(1024)}, /*index=5*/f32[768]{0:T(1024)}) all-reduce(f32[768]{0:T(1024)S(1)} %copy-done.30, f32[768]{0:T(1024)S(1)} %get-tuple-element.121, f32[768]{0:T(1024)S(1)} %copy-done.32, ...), channel_id=1, replica_groups=mesh['dp'=16,'tensor'=2] {'dp','tensor'}, use_global_device_ids=true, to_apply=%region_24.25 | all-reduce | flops 4608 | bytes 36864 | tf_op jit(solution)/shard_map/psum | solution.py:263
  516.5 76.6 %all-reduce.2 = (f32[2,384]{1,0:T(2,128)}, f32[1536]{0:T(1024)}) all-reduce(f32[2,384]{1,0:T(2,128)S(1)} %pad_maximum_fusion.10, f32[1536]{0:T(1024)S(1)} %copy-done.34), channel_id=1, replica_groups=mesh['dp'=16,'tensor'=2] {'dp'}, use_global_device_ids=true, to_apply=%region_21.22 | all-reduce | flops 2304 | bytes 18432 | tf_op jit(solution)/shard_map/psum | solution.py:255
  593.1 2.3 add_convert_fusion.2
  595.4 54.9 %all-reduce.5.cloned.1.call-done = f32[3,768,384]{2,0,1:T(4,128)} async-done(((f32[3,768,384]{2,0,1:T(4,128)}), f32[3,768,384]{2,0,1:T(4,128)}) %all-reduce.5.cloned.1.call-update) | async-done | bytes 3538960
  652.0 8.6 reduce-scatter.20.cloned.1.call-done
  660.6 141.8 %reduce-scatter.18.cloned.1.call-done = f32[48,1536]{1,0:T(8,128)} async-done(((f32[768,1536]{1,0:T(8,128)}), f32[48,1536]{1,0:T(8,128)}) %reduce-scatter.18.cloned.1.call-update) | async-done | bytes 294928 | tf_op jit(solution)/shard_map/reduce_scatter | solution.py:252
  802.4 128.8 %reduce-scatter.16.cloned.1.call-done = f32[384,48]{0,1:T(8,128)} async-done(((f32[384,768]{0,1:T(8,128)}), f32[384,48]{0,1:T(8,128)}) %reduce-scatter.16.cloned.1.call-update) | async-done | bytes 73744 | tf_op jit(solution)/shard_map/reduce_scatter | solution.py:251
  (171 shorter events, 21.5 us)
Async XLA Ops:
  8.0 29.9 %copy-start.20 = (bf16[3,48,384]{2,1,0:T(8,128)(2,1)S(1)}, bf16[3,48,384]{2,1,0:T(8,128)(2,1)}, u32[]{:S(2)}) copy-start(bf16[3,48,384]{2,1,0:T(8,128)(2,1)} %param.17) | copy-start | bytes 331780
  8.0 29.2 %copy-start.39 = (f32[2,384]{1,0:T(2,128)S(1)}, f32[2,384]{1,0:T(2,128)}, u32[]{:S(2)}) copy-start(f32[2,384]{1,0:T(2,128)} %param.18) | copy-start | bytes 9220
  8.0 30.6 %copy-start.28 = (bf16[384,48]{0,1:T(8,128)(2,1)S(1)}, bf16[384,48]{0,1:T(8,128)(2,1)}, u32[]{:S(2)}) copy-start(bf16[384,48]{0,1:T(8,128)(2,1)} %param.19) | copy-start | bytes 110596
  8.0 100.0 %all-gather.7.cloned.1.call-start = ((), (), s32[]{:S(2)}) async-start(), calls=%async_computation.7 | async-start | bytes 2359296 | tf_op jit(solution)/shard_map/all_gather | solution.py:82
  8.1 9.6 %collective-permute-start = (bf16[3,48,384]{2,1,0:T(8,128)(2,1)}, bf16[3,48,384]{2,1,0:T(8,128)(2,1)S(1)}, u32[]{:S(2)}, u32[]{:S(2)}) collective-permute-start(bf16[3,48,384]{2,1,0:T(8,128)(2,1)} %param.17), channel_id=1, source_target_pairs={{0,30},{2,0},{4,2},{6,4},{8,6},{10,8},{12,10},{14,12},{16,14},{18,... | collective-permute-start | bytes 331784 | tf_op jit(solution)/shard_map/ppermute | solution.py:72
  18.6 6.4 collective-permute-start.1
  26.0 10.2 %collective-permute-start.2 = (bf16[3,192,384]{2,1,0:T(8,128)(2,1)S(1)}, bf16[3,192,384]{2,1,0:T(8,128)(2,1)S(1)}, u32[]{:S(2)}, u32[]{:S(2)}) collective-permute-start(bf16[3,192,384]{2,1,0:T(8,128)(2,1)S(1)} %pad_maximum_fusion.6), channel_id=1, source_target_pairs={{0,24},{2,26},{4,28},{6,30},{8,0},{10,2},{12,4},{14,6},{16,8},{18,... | collective-permute-start | bytes 1327112 | tf_op jit(solution)/shard_map/ppermute | solution.py:72
  26.5 131.5 %reduce-scatter.8.cloned.1.call-start = ((), (), s32[]{:S(2)}) async-start(), calls=%async_computation.8 | async-start | bytes 4718592 | tf_op jit(solution)/shard_map/reduce_scatter | solution.py:125
  37.1 66.0 %collective-permute-start.3 = (bf16[3,384,384]{2,1,0:T(8,128)(2,1)S(1)}, bf16[3,384,384]{2,1,0:T(8,128)(2,1)S(1)}, u32[]{:S(2)}, u32[]{:S(2)}) collective-permute-start(bf16[3,384,384]{2,1,0:T(8,128)(2,1)S(1)} %pad_maximum_fusion.1), channel_id=1, source_target_pairs={{0,16},{2,18},{4,20},{6,22},{8,24},{10,26},{12,28},{14,30},{16,0},... | collective-permute-start | bytes 2654216 | tf_op jit(solution)/shard_map/ppermute | solution.py:72
  108.0 2.6 copy-start.41
  110.6 4.1 copy-start.6
  110.6 4.1 copy-start.8
  112.8 1.9 copy-start.4
  114.7 16.3 %copy-start = (f32[6,512,1024]{2,1,0:T(8,128)}, f32[6,512,1024]{2,1,0:T(8,128)S(1)}, u32[]{:S(2)}) copy-start(f32[6,512,1024]{2,1,0:T(8,128)S(1)} %fusion.64) | copy-start | bytes 37748740
  119.6 7.6 copy-start.1
  119.6 5.7 copy-start.42
  127.2 3.8 copy-start.18
  131.0 3.8 copy-start.23
  131.1 4.5 copy-start.21
  135.6 22.4 %copy-start.15 = (bf16[512,768]{1,0:T(8,128)(2,1)S(1)}, bf16[512,768]{1,0:T(8,128)(2,1)}, u32[]{:S(2)}) copy-start(bf16[512,768]{1,0:T(8,128)(2,1)} %param.15) | copy-start | bytes 2359300
  135.6 22.4 %copy-start.37 = (f32[768]{0:T(1024)S(1)}, f32[768]{0:T(1024)}, u32[]{:S(2)}) copy-start(f32[768]{0:T(1024)} %param.20) | copy-start | bytes 9220
  138.4 21.6 %copy-start.27 = (f32[768]{0:T(1024)S(1)}, f32[768]{0:T(1024)}, u32[]{:S(2)}) copy-start(f32[768]{0:T(1024)} %param.25) | copy-start | bytes 9220
  138.4 21.6 %copy-start.31 = (f32[768]{0:T(1024)S(1)}, f32[768]{0:T(1024)}, u32[]{:S(2)}) copy-start(f32[768]{0:T(1024)} %param.26) | copy-start | bytes 9220
  138.4 74.7 %all-gather.11.cloned.1.call-start = ((), (), s32[]{:S(2)}) async-start(), calls=%async_computation.10 | async-start | bytes 2506752 | tf_op jit(solution)/shard_map/all_gather | solution.py:79
  139.0 84.2 %copy-start.45 = (f32[1536]{0:T(1024)S(1)}, f32[1536]{0:T(1024)}, u32[]{:S(2)}) copy-start(f32[1536]{0:T(1024)} %param.22) | copy-start | bytes 18436
  139.0 84.2 %all-gather.9.cloned.1.call-start = ((), (), s32[]{:S(2)}) async-start(), calls=%async_computation.9 | async-start | bytes 2359296 | tf_op jit(solution)/shard_map/all_gather | solution.py:131
  161.3 128.7 %all-gather.13.cloned.1.call-start = ((), (), s32[]{:S(2)}) async-start(), calls=%async_computation.11 | async-start | bytes 2506752 | tf_op jit(solution)/shard_map/all_gather | solution.py:80
  161.8 144.4 %reduce-scatter.10.cloned.1.call-start = ((), (), s32[]{:S(2)}) async-start(), calls=%async_computation.12 | async-start | bytes 4718592 | tf_op jit(solution)/shard_map/reduce_scatter | solution.py:136
  290.0 16.2 %copy-start.38 = (f32[768]{0:T(1024)S(1)}, f32[768]{0:T(1024)}, u32[]{:S(2)}) copy-start(f32[768]{0:T(1024)} %param.24) | copy-start | bytes 9220
  296.9 11.6 %copy-start.14 = (bf16[512,768]{1,0:T(8,128)(2,1)S(1)}, bf16[512,768]{1,0:T(8,128)(2,1)}, u32[]{:S(2)}) copy-start(bf16[512,768]{1,0:T(8,128)(2,1)} %param.29) | copy-start | bytes 2359300
  296.9 11.6 %copy-start.29 = (f32[768]{0:T(1024)S(1)}, f32[768]{0:T(1024)}, u32[]{:S(2)}) copy-start(f32[768]{0:T(1024)} %param.27) | copy-start | bytes 9220
  296.9 12.3 %copy-start.35 = (f32[768]{0:T(1024)S(1)}, f32[768]{0:T(1024)}, u32[]{:S(2)}) copy-start(f32[768]{0:T(1024)} %param.28) | copy-start | bytes 9220
  296.9 27.2 %all-gather.15.cloned.1.call-start = ((), (), s32[]{:S(2)}) async-start(), calls=%async_computation.13 | async-start | bytes 2359296 | tf_op jit(solution)/shard_map/all_gather | solution.py:146
  313.1 40.0 %reduce-scatter.12.cloned.1.call-start = ((), (), s32[]{:S(2)}) async-start(), calls=%async_computation.14 | async-start | bytes 4718592 | tf_op jit(solution)/shard_map/reduce_scatter | solution.py:154
  324.1 12.6 %copy-start.40 = (bf16[768,1536]{1,0:T(8,128)(2,1)S(1)}, bf16[768,1536]{1,0:T(8,128)(2,1)}, u32[]{:S(2)}) copy-start(bf16[768,1536]{1,0:T(8,128)(2,1)} %all-gather.11.cloned.1.call-done) | copy-start | bytes 7077892
  335.0 1.7 copy-start.16
  341.1 29.6 %all-gather.17.cloned.1.call-start = ((), (), s32[]{:S(2)}) async-start(), calls=%async_computation.15 | async-start | bytes 2359296 | tf_op jit(solution)/shard_map/all_gather | solution.py:161
  355.9 14.7 %copy-start.22 = (bf16[384,768]{0,1:T(8,128)(2,1)S(1)}, bf16[384,768]{0,1:T(8,128)(2,1)}, u32[]{:S(2)}) copy-start(bf16[384,768]{0,1:T(8,128)(2,1)} %all_gather.22) | copy-start | bytes 1769476
  359.4 13.5 %copy-start.19 = (bf16[384,1024]{1,0:T(8,128)(2,1)S(1)}, bf16[384,1024]{1,0:T(8,128)(2,1)}, u32[]{:S(2)}) copy-start(bf16[384,1024]{1,0:T(8,128)(2,1)} %copy-done.18) | copy-start | bytes 2359300
  359.5 233.7 %reduce-scatter.14.cloned.1.call-start = ((), (), s32[]{:S(2)}) async-start(), calls=%async_computation.16 | async-start | bytes 2359296 | tf_op jit(solution)/shard_map/reduce_scatter | solution.py:238
  406.1 17.3 %copy-start.5 = (bf16[384,1024]{1,0:T(8,128)(2,1)S(1)}, bf16[384,1024]{1,0:T(8,128)(2,1)}, u32[]{:S(2)}) copy-start(bf16[384,1024]{1,0:T(8,128)(2,1)} %copy-done.4) | copy-start | bytes 2359300
  423.4 2.0 copy-start.9
  423.4 5.3 slice-start
  425.5 17.0 %copy-start.10 = (bf16[6,64,512]{2,1,0:T(8,128)(2,1)}, bf16[6,64,512]{2,1,0:T(8,128)(2,1)S(1)}, u32[]{:S(2)}) copy-start(bf16[6,64,512]{2,1,0:T(8,128)(2,1)S(1)} %fusion.28) | copy-start | bytes 1179652
  425.5 3.3 slice-start.1
  425.5 3.6 slice-start.2
  426.7 2.9 copy-start.47
  429.7 12.8 %copy-start.12 = (bf16[6,64,512]{2,1,0:T(8,128)(2,1)}, bf16[6,64,512]{2,1,0:T(8,128)(2,1)S(1)}, u32[]{:S(2)}) copy-start(bf16[6,64,512]{2,1,0:T(8,128)(2,1)S(1)} %fusion.29) | copy-start | bytes 1179652
  429.7 4.0 copy-start.7
  442.4 207.9 %all-reduce.5.cloned.1.call-start = ((), (), s32[]{:S(2)}) async-start(), calls=%async_computation.20 | async-start | bytes 9437184
  442.5 2.3 copy-start.43
  450.7 209.9 %reduce-scatter.20.cloned.1.call-start = ((), (), s32[]{:S(2)}) async-start(), calls=%async_computation.19 | async-start | bytes 5013504 | tf_op jit(solution)/shard_map/reduce_scatter | solution.py:253
  458.5 1.9 copy-start.17
  458.5 343.8 %reduce-scatter.18.cloned.1.call-start = ((), (), s32[]{:S(2)}) async-start(), calls=%async_computation.18 | async-start | bytes 5013504 | tf_op jit(solution)/shard_map/reduce_scatter | solution.py:252
  466.3 4.7 copy-start.46
  466.3 6.0 copy-start.30
  466.3 6.0 copy-start.32
  466.3 6.0 copy-start.33
  466.3 49.9 %copy-start.11 = (bf16[6,64,512]{2,1,0:T(8,128)(2,1)S(1)}, bf16[6,64,512]{2,1,0:T(8,128)(2,1)}, u32[]{:S(2)}) copy-start(bf16[6,64,512]{2,1,0:T(8,128)(2,1)} %copy-done.10) | copy-start | bytes 1179652
  466.3 49.9 %copy-start.13 = (bf16[6,64,512]{2,1,0:T(8,128)(2,1)S(1)}, bf16[6,64,512]{2,1,0:T(8,128)(2,1)}, u32[]{:S(2)}) copy-start(bf16[6,64,512]{2,1,0:T(8,128)(2,1)} %copy-done.12) | copy-start | bytes 1179652
  466.3 50.0 %copy-start.36 = (f32[6,64]{1,0:T(8,128)S(1)}, f32[6,64]{1,0:T(8,128)}, u32[]{:S(2)}) copy-start(f32[6,64]{1,0:T(8,128)} %get-tuple-element.148) | copy-start | bytes 4612
  466.3 50.1 %copy-start.34 = (f32[1536]{0:T(1024)S(1)}, f32[1536]{0:T(1024)}, u32[]{:S(2)}) copy-start(f32[1536]{0:T(1024)} %get-tuple-element.125) | copy-start | bytes 18436
  466.3 126.8 %copy-start.3 = (f32[512,768]{1,0:T(8,128)S(1)}, f32[512,768]{1,0:T(8,128)}, u32[]{:S(2)}) copy-start(f32[512,768]{1,0:T(8,128)} %copy-done.2) | copy-start | bytes 4718596
  466.4 464.8 %reduce-scatter.16.cloned.1.call-start = ((), (), s32[]{:S(2)}) async-start(), calls=%async_computation.17 | async-start | bytes 1253376 | tf_op jit(solution)/shard_map/reduce_scatter | solution.py:251
  (5 other events, 5.5 us)
Sparse Core Ops, SparseCore 0:
  26.6 14.3 all-gather.6
  138.5 19.4 reduce-scatter.7
  297.0 9.1 reduce-scatter.9
  359.6 11.0 all-gather.16
  442.5 10.2 reduce-scatter.13
  459.2 201.3 reduce-scatter.19
  666.3 136.0 reduce-scatter.17
  808.4 122.7 reduce-scatter.15
Sparse Core Ops, SparseCore 1:
  142.1 71.0 all-gather.10
  215.2 7.9 all-gather.8
  226.2 63.7 all-gather.12
  313.2 10.8 all-gather.14
  341.1 11.9 reduce-scatter.11
  450.7 199.5 all-reduce.4
